TPU v7x, 32 devices: a whole 2x2x4 slice. The times are simulated.
32 devices in a mesh: seg: 2 (over y), gx: 8 (over z, x), gy: 2 (over core).
Axes of the slice: x: 2, y: 2, z: 4, core: 2. Of those that a mesh axis runs over, the one named last changes fastest.
Arguments:
- populations: float32 [52, 64, 64, 128], P('seg', 'gx', 'gy'), parts along dimension 0, may hold values from 0 to 1, as said below
- cell_flags: int32 [64, 64, 256], P('gx', 'gy', 'seg'), parts along dimension 2, may hold values from 0 to 3, as said below
Outputs:
- fields: float32 [10, 64, 64, 128], P('seg', 'gx', 'gy'), parts along dimension 0
There are 2 independent parts, one for each index of `seg`. A program takes and returns all parts, laid end to end along the dimension named above; each array names one. Nothing has to cross between parts.
Inputs may be any that keep to these rules, and one draw needn't show every extreme that they name: `populations`: populations are positive and near a local equilibrium of each cell. `cell_flags`: the value 2 is added only on the first and last plane along the channel height.
All inputs are finite; a program needn't handle non-finite values.
Results may differ from a plain program's by a relative error of at most 0.0001.
Values sent between devices are 32-bit elements; how exact they have to be, the bound alone decides.
A program may use at most 64 MiB of HBM per device.

v0:
```python
import jax
import jax.numpy as jnp
from jax import lax
from jax.sharding import PartitionSpec as P

STEPS = 3


VELOCITY = [
    (0, 0, 0),
    (1, 0, 0),
    (-1, 0, 0),
    (0, 1, 0),
    (0, -1, 0),
    (0, 0, 1),
    (0, 0, -1),
    (1, 1, 0),
    (-1, -1, 0),
    (1, -1, 0),
    (-1, 1, 0),
    (1, 0, 1),
    (-1, 0, -1),
    (1, 0, -1),
    (-1, 0, 1),
    (0, 1, 1),
    (0, -1, -1),
    (0, 1, -1),
    (0, -1, 1),
]
FLOW_WEIGHT = [1.0 / 3.0] + [1.0 / 18.0] * 6 + [1.0 / 36.0] * 12
SALT_WEIGHT = [0.25] + [0.125] * 6
tau_plus = 0.65
tau_minus = 0.5 + 0.25 / (tau_plus - 0.5)
salt_minus = 0.7
salt_plus = 0.5 + 0.25 / (salt_minus - 0.5)
speed_scale = 0.1


def extended_2(value, sides, width):
    for axis, dim in sides:
        size, length = (lax.axis_size(axis), value.shape[dim])
        up = [(i, (i + 1) % size) for i in range(size)]
        down = [(j, i) for i, j in up]
        last = lax.slice_in_dim(value, length - width, length, axis=dim)
        initial = lax.slice_in_dim(value, 0, width, axis=dim)
        before = lax.ppermute(last, axis, up)
        after = lax.ppermute(initial, axis, down)
        value = jnp.concatenate([before, value, after], axis=dim)
    return value


def partner(index):
    if index == 0:
        return 0
    return index + 1 if index % 2 == 1 else index - 1


def lattice_vector(index):
    return VELOCITY[index] if index < 19 else VELOCITY[index - 19]


def opposite_of(index):
    return partner(index) if index < 19 else 19 + partner(index - 19)


def component(pops, first, axis):
    total = None
    for offset in range(len(pops)):
        sign = lattice_vector(first + offset)[axis]
        if sign != 0:
            term = pops[offset] if sign > 0 else -pops[offset]
            total = term if total is None else total + term
    return total


def collide(state, flags):
    solid_mask = flags % 2 == 1
    open_wall = (flags // 2).astype(jnp.float32) * (1.0 - solid_mask.astype(jnp.float32))
    flow = [state[q] for q in range(19)]
    salt = [state[19 + k] for k in range(7)]
    density = sum(flow[1:], flow[0])
    speeds = [component(flow, 0, a) / density for a in range(3)]
    usq = speeds[0] * speeds[0] + speeds[1] * speeds[1] + speeds[2] * speeds[2]
    post = [None] * 26
    post[0] = flow[0] - (flow[0] - density * (1.0 - 1.5 * usq) / 3.0) / tau_plus
    for q in range(1, 19, 2):
        other = q + 1
        vec = VELOCITY[q]
        along = vec[0] * speeds[0] + vec[1] * speeds[1] + vec[2] * speeds[2]
        weight = FLOW_WEIGHT[q]
        even_eq = weight * density * (1.0 + 4.5 * along * along - 1.5 * usq)
        odd_eq = 3.0 * weight * density * along
        dplus = (0.5 * (flow[q] + flow[other]) - even_eq) / tau_plus
        dminus = (0.5 * (flow[q] - flow[other]) - odd_eq) / tau_minus
        post[q] = flow[q] - dplus - dminus
        post[other] = flow[other] - dplus + dminus
    conc = sum(salt[1:], salt[0])
    post[19] = salt[0] - (salt[0] - 0.25 * conc) / salt_plus
    for k in range(1, 7, 2):
        other = k + 1
        vec = VELOCITY[k]
        along = vec[0] * speeds[0] + vec[1] * speeds[1] + vec[2] * speeds[2]
        weight = SALT_WEIGHT[k]
        even_eq = weight * conc
        odd_eq = 4.0 * weight * conc * along
        dplus = (0.5 * (salt[k] + salt[other]) - even_eq) / salt_plus
        dminus = (0.5 * (salt[k] - salt[other]) - odd_eq) / salt_minus
        post[19 + k] = salt[k] - dplus - dminus
        post[19 + other] = salt[other] - dplus + dminus
    post = [jnp.where(solid_mask, state[opposite_of(q)], post[q]) for q in range(26)]
    rate = 0.03 * (1.5 - 0.5 * conc) * open_wall
    flow_loss = 6.0 * density * rate
    salt_loss = 0.02 * conc * open_wall
    return (jnp.stack(post), flow_loss, salt_loss)


def slide_xy(extended):
    span_x = extended.shape[1] - 2
    span_y = extended.shape[2] - 2
    moved = []
    for q in range(26):
        vec = lattice_vector(q)
        moved.append(
            extended[q, 1 - vec[0] : 1 - vec[0] + span_x, 1 - vec[1] : 1 - vec[1] + span_y]
        )
    return moved


def finish(moved, inner, flow_loss, salt_loss):
    parts = []
    for q in range(26):
        rise = lattice_vector(q)[2]
        source = moved[q]
        if rise == 0:
            parts.append(source)
            continue
        loss = flow_loss * FLOW_WEIGHT[q] if q < 19 else salt_loss
        if rise == 1:
            entering = inner[opposite_of(q)][:, :, :1] - loss[:, :, :1]
            parts.append(jnp.concatenate([entering, source[:, :, :-1]], axis=2))
        else:
            entering = inner[opposite_of(q)][:, :, -1:] - loss[:, :, -1:]
            parts.append(jnp.concatenate([source[:, :, 1:], entering], axis=2))
    return jnp.stack(parts)


def moments(state):
    flow = [state[q] for q in range(19)]
    salt = [state[19 + k] for k in range(7)]
    density = sum(flow[1:], flow[0])
    momenta = [component(flow, 0, a) / speed_scale for a in range(3)]
    conc = sum(salt[1:], salt[0])
    return jnp.stack([density] + momenta + [conc])


def per_device(populations, cell_flags):
    state = populations
    for step in range(STEPS):
        post, flow_loss, salt_loss = collide(state, cell_flags)
        extended = extended_2(post, (("gx", 1), ("gy", 2)), 1)
        moved = slide_xy(extended)
        state = finish(moved, post, flow_loss, salt_loss)
    return moments(state)


def solution(mesh):
    return jax.shard_map(
        per_device,
        mesh=mesh,
        in_specs=(P("seg", "gx", "gy", None), P("gx", "gy", "seg")),
        out_specs=P("seg", "gx", "gy", None),
        check_vma=False,
    )
```

profile of v0, /device:TPU:0, one launch (start us, length us, event | category | flops | bytes accessed | tf_op | source)
XLA Modules:
  0.0 91.5 jit_solution(9620247091789317802)
XLA Ops:
  0.0 2.6 %broadcast_multiply_fusion.10 = (f32[8,32,128]{2,1,0:T(8,128)S(1)}, f32[8,32,128]{2,1,0:T(8,128)S(1)}, f32[8,32,128]{2,1,0:T(8,128)S(1)}, pred[8,32,128]{2,1,0:T(8,128)(4,1)S(1)}) fusion(s32[8,32,128]{2,1,0:T(8,128)} %param.3, f32[26,8,32,128]{3,2,1,0:T(8,128)} %param.2), kind=kLoop, calls=%fused_computation.790 | loop fusion | flops 1802240 | bytes 3964928 | tf_op jit(solution)/shard_map/mul | solution.py:137
  2.6 0.5 copy-done
  3.1 0.3 constant_dynamic-update-slice_fusion.25
  3.7 0.1 constant_dynamic-update-slice_fusion.22
  3.9 0.1 constant_dynamic-update-slice_fusion.20
  4.4 0.1 constant_dynamic-update-slice_fusion.16
  4.5 0.1 constant_dynamic-update-slice_fusion.15
  6.2 3.0 %collective-permute-start = (f32[26,1,32,128]{3,2,1,0:T(8,128)S(1)}, f32[26,1,32,128]{3,2,1,0:T(8,128)S(1)}, u32[]{:S(2)}, u32[]{:S(2)}) collective-permute-start(f32[26,1,32,128]{3,2,1,0:T(8,128)S(1)} %get-tuple-element.226), channel_id=1, source_target_pairs={{0,2},{2,4},{4,6},{6,8},{8,10},{10,12},{12,14},{14,0},{1,3},{3,5},... | collective-permute-start | bytes 1277960 | tf_op jit(solution)/shard_map/ppermute | solution.py:46
  9.2 3.1 %collective-permute-start.1 = (f32[26,1,32,128]{3,2,1,0:T(8,128)S(1)}, f32[26,1,32,128]{3,2,1,0:T(8,128)S(1)}, u32[]{:S(2)}, u32[]{:S(2)}) collective-permute-start(f32[26,1,32,128]{3,2,1,0:T(8,128)S(1)} %get-tuple-element.225), channel_id=1, source_target_pairs={{2,0},{4,2},{6,4},{8,6},{10,8},{12,10},{14,12},{0,14},{3,1},{5,3},... | collective-permute-start | bytes 1277960 | tf_op jit(solution)/shard_map/ppermute | solution.py:47
  12.3 0.1 broadcast_multiply_fusion.7
  12.4 0.1 slice_subtract_fusion.25
  12.6 0.3 slice_subtract_fusion.26
  12.8 14.6 %collective-permute-done = f32[26,1,32,128]{3,2,1,0:T(8,128)S(1)} collective-permute-done((f32[26,1,32,128]{3,2,1,0:T(8,128)S(1)}, f32[26,1,32,128]{3,2,1,0:T(8,128)S(1)}, u32[]{:S(2)}, u32[]{:S(2)}) %collective-permute-start) | collective-permute-done | bytes 426016 | tf_op jit(solution)/shard_map/ppermute | solution.py:46
  27.4 2.2 %collective-permute-done.1 = f32[26,1,32,128]{3,2,1,0:T(8,128)S(1)} collective-permute-done((f32[26,1,32,128]{3,2,1,0:T(8,128)S(1)}, f32[26,1,32,128]{3,2,1,0:T(8,128)S(1)}, u32[]{:S(2)}, u32[]{:S(2)}) %collective-permute-start.1) | collective-permute-done | bytes 426016 | tf_op jit(solution)/shard_map/ppermute | solution.py:47
  29.6 0.2 pad_maximum_fusion.6
  29.9 0.5 collective-permute-start.3
  30.4 0.1 slice_subtract_fusion.34
  30.9 0.3 collective-permute-done.2
  31.2 0.2 collective-permute-done.3
  31.7 0.2 multiply_multiply_fusion.29
  31.9 0.6 broadcast_multiply_fusion.5
  32.5 0.1 broadcast_multiply_fusion.9
  32.7 0.3 constant_dynamic-update-slice_fusion.51
  33.0 0.1 constant_dynamic-update-slice_fusion.50
  33.3 0.1 constant_dynamic-update-slice_fusion.48
  33.5 0.1 constant_dynamic-update-slice_fusion.46
  35.5 0.2 constant_dynamic-update-slice_fusion.27
  35.7 0.2 constant_dynamic-update-slice_fusion.26
  35.9 0.3 collective-permute-start.4
  36.3 4.4 %collective-permute-start.5 = (f32[26,1,32,128]{3,2,1,0:T(8,128)S(1)}, f32[26,1,32,128]{3,2,1,0:T(8,128)S(1)}, u32[]{:S(2)}, u32[]{:S(2)}) collective-permute-start(f32[26,1,32,128]{3,2,1,0:T(8,128)S(1)} %get-tuple-element.222), channel_id=1, source_target_pairs={{2,0},{4,2},{6,4},{8,6},{10,8},{12,10},{14,12},{0,14},{3,1},{5,3},... | collective-permute-start | bytes 1277960 | tf_op jit(solution)/shard_map/ppermute | solution.py:47
  40.7 0.1 slice_subtract_fusion.22
  40.8 0.3 slice_subtract_fusion.14
  41.1 13.8 %collective-permute-done.4 = f32[26,1,32,128]{3,2,1,0:T(8,128)S(1)} collective-permute-done((f32[26,1,32,128]{3,2,1,0:T(8,128)S(1)}, f32[26,1,32,128]{3,2,1,0:T(8,128)S(1)}, u32[]{:S(2)}, u32[]{:S(2)}) %collective-permute-start.4) | collective-permute-done | bytes 426016 | tf_op jit(solution)/shard_map/ppermute | solution.py:46
  55.0 2.9 %collective-permute-done.5 = f32[26,1,32,128]{3,2,1,0:T(8,128)S(1)} collective-permute-done((f32[26,1,32,128]{3,2,1,0:T(8,128)S(1)}, f32[26,1,32,128]{3,2,1,0:T(8,128)S(1)}, u32[]{:S(2)}, u32[]{:S(2)}) %collective-permute-start.5) | collective-permute-done | bytes 426016 | tf_op jit(solution)/shard_map/ppermute | solution.py:47
  57.9 0.2 pad_maximum_fusion.3
  58.1 0.5 collective-permute-start.7
  58.6 0.1 slice_subtract_fusion.13
  59.2 0.3 collective-permute-done.6
  59.5 0.2 collective-permute-done.7
  59.9 0.2 multiply_multiply_fusion.27
  60.1 0.6 broadcast_multiply_fusion.3
  60.8 0.1 broadcast_multiply_fusion.8
  60.9 0.3 constant_dynamic-update-slice_fusion.77
  61.3 0.1 constant_dynamic-update-slice_fusion.76
  61.5 0.1 constant_dynamic-update-slice_fusion.74
  61.7 0.1 constant_dynamic-update-slice_fusion.72
  63.8 0.2 constant_dynamic-update-slice_fusion.53
  63.9 0.2 constant_dynamic-update-slice_fusion.52
  64.2 4.7 %collective-permute-start.9 = (f32[26,1,32,128]{3,2,1,0:T(8,128)S(1)}, f32[26,1,32,128]{3,2,1,0:T(8,128)S(1)}, u32[]{:S(2)}, u32[]{:S(2)}) collective-permute-start(f32[26,1,32,128]{3,2,1,0:T(8,128)S(1)} %get-tuple-element.219), channel_id=1, source_target_pairs={{2,0},{4,2},{6,4},{8,6},{10,8},{12,10},{14,12},{0,14},{3,1},{5,3},... | collective-permute-start | bytes 1277960 | tf_op jit(solution)/shard_map/ppermute | solution.py:47
  69.0 0.1 slice_subtract_fusion
  69.2 0.1 slice_subtract_fusion.10
  69.5 0.3 slice_subtract_fusion.2
  69.7 13.5 %collective-permute-done.8 = f32[26,1,32,128]{3,2,1,0:T(8,128)S(1)} collective-permute-done((f32[26,1,32,128]{3,2,1,0:T(8,128)S(1)}, f32[26,1,32,128]{3,2,1,0:T(8,128)S(1)}, u32[]{:S(2)}, u32[]{:S(2)}) %collective-permute-start.8) | collective-permute-done | bytes 426016 | tf_op jit(solution)/shard_map/ppermute | solution.py:46
  83.2 3.1 %collective-permute-done.9 = f32[26,1,32,128]{3,2,1,0:T(8,128)S(1)} collective-permute-done((f32[26,1,32,128]{3,2,1,0:T(8,128)S(1)}, f32[26,1,32,128]{3,2,1,0:T(8,128)S(1)}, u32[]{:S(2)}, u32[]{:S(2)}) %collective-permute-start.9) | collective-permute-done | bytes 426016 | tf_op jit(solution)/shard_map/ppermute | solution.py:47
  86.3 0.2 pad_maximum_fusion
  86.6 0.5 collective-permute-start.11
  87.3 0.6 collective-permute-done.10
  87.9 0.2 collective-permute-done.11
  88.4 0.5 constant_dynamic-update-slice_fusion.82
  89.0 0.2 constant_dynamic-update-slice_fusion.81
  89.2 0.2 constant_dynamic-update-slice_fusion.80
  89.4 0.4 constant_dynamic-update-slice_fusion.79
  89.9 0.8 copy-done.2
  90.7 0.8 constant_dynamic-update-slice_fusion.78
  (97 shorter events, 8.6 us)
Async XLA Ops:
  0.0 3.1 %copy-start = (f32[26,8,32,128]{3,2,1,0:T(8,128)S(1)}, f32[26,8,32,128]{3,2,1,0:T(8,128)}, u32[]{:S(2)}) copy-start(f32[26,8,32,128]{3,2,1,0:T(8,128)} %param.2) | copy-start | bytes 10223620
  5.6 6.7 %copy-start.1 = (s32[8,32,128]{2,1,0:T(8,128)S(1)}, s32[8,32,128]{2,1,0:T(8,128)}, u32[]{:S(2)}) copy-start(s32[8,32,128]{2,1,0:T(8,128)} %param.3) | copy-start | bytes 393220
  6.2 21.2 %collective-permute-start = (f32[26,1,32,128]{3,2,1,0:T(8,128)S(1)}, f32[26,1,32,128]{3,2,1,0:T(8,128)S(1)}, u32[]{:S(2)}, u32[]{:S(2)}) collective-permute-start(f32[26,1,32,128]{3,2,1,0:T(8,128)S(1)} %get-tuple-element.226), channel_id=1, source_target_pairs={{0,2},{2,4},{4,6},{6,8},{8,10},{10,12},{12,14},{14,0},{1,3},{3,5},... | collective-permute-start | bytes 1277960 | tf_op jit(solution)/shard_map/ppermute | solution.py:46
  9.2 20.4 %collective-permute-start.1 = (f32[26,1,32,128]{3,2,1,0:T(8,128)S(1)}, f32[26,1,32,128]{3,2,1,0:T(8,128)S(1)}, u32[]{:S(2)}, u32[]{:S(2)}) collective-permute-start(f32[26,1,32,128]{3,2,1,0:T(8,128)S(1)} %get-tuple-element.225), channel_id=1, source_target_pairs={{2,0},{4,2},{6,4},{8,6},{10,8},{12,10},{14,12},{0,14},{3,1},{5,3},... | collective-permute-start | bytes 1277960 | tf_op jit(solution)/shard_map/ppermute | solution.py:47
  29.8 1.4 %collective-permute-start.2 = (f32[26,10,1,128]{3,2,1,0:T(1,128)S(1)}, f32[26,10,1,128]{3,2,1,0:T(1,128)S(1)}, u32[]{:S(2)}, u32[]{:S(2)}) collective-permute-start(f32[26,10,1,128]{3,2,1,0:T(1,128)S(1)} %get-tuple-element.208), channel_id=1, source_target_pairs={{0,1},{1,0},{2,3},{3,2},{4,5},{5,4},{6,7},{7,6},{8,9},{9,8},{10,11... | collective-permute-start | bytes 399368 | tf_op jit(solution)/shard_map/ppermute | solution.py:46
  29.9 1.5 %collective-permute-start.3 = (f32[26,10,1,128]{3,2,1,0:T(1,128)S(1)}, f32[26,10,1,128]{3,2,1,0:T(1,128)S(1)}, u32[]{:S(2)}, u32[]{:S(2)}) collective-permute-start(f32[26,10,1,128]{3,2,1,0:T(1,128)S(1)} %get-tuple-element.207), channel_id=1, source_target_pairs={{1,0},{0,1},{3,2},{2,3},{5,4},{4,5},{7,6},{6,7},{9,8},{8,9},{11,10... | collective-permute-start | bytes 399368 | tf_op jit(solution)/shard_map/ppermute | solution.py:47
  35.9 19.0 %collective-permute-start.4 = (f32[26,1,32,128]{3,2,1,0:T(8,128)S(1)}, f32[26,1,32,128]{3,2,1,0:T(8,128)S(1)}, u32[]{:S(2)}, u32[]{:S(2)}) collective-permute-start(f32[26,1,32,128]{3,2,1,0:T(8,128)S(1)} %get-tuple-element.223), channel_id=1, source_target_pairs={{0,2},{2,4},{4,6},{6,8},{8,10},{10,12},{12,14},{14,0},{1,3},{3,5},... | collective-permute-start | bytes 1277960 | tf_op jit(solution)/shard_map/ppermute | solution.py:46
  36.3 21.6 %collective-permute-start.5 = (f32[26,1,32,128]{3,2,1,0:T(8,128)S(1)}, f32[26,1,32,128]{3,2,1,0:T(8,128)S(1)}, u32[]{:S(2)}, u32[]{:S(2)}) collective-permute-start(f32[26,1,32,128]{3,2,1,0:T(8,128)S(1)} %get-tuple-element.222), channel_id=1, source_target_pairs={{2,0},{4,2},{6,4},{8,6},{10,8},{12,10},{14,12},{0,14},{3,1},{5,3},... | collective-permute-start | bytes 1277960 | tf_op jit(solution)/shard_map/ppermute | solution.py:47
  58.0 1.4 %collective-permute-start.6 = (f32[26,10,1,128]{3,2,1,0:T(1,128)S(1)}, f32[26,10,1,128]{3,2,1,0:T(1,128)S(1)}, u32[]{:S(2)}, u32[]{:S(2)}) collective-permute-start(f32[26,10,1,128]{3,2,1,0:T(1,128)S(1)} %get-tuple-element.204), channel_id=1, source_target_pairs={{0,1},{1,0},{2,3},{3,2},{4,5},{5,4},{6,7},{7,6},{8,9},{9,8},{10,11... | collective-permute-start | bytes 399368 | tf_op jit(solution)/shard_map/ppermute | solution.py:46
  58.1 1.5 %collective-permute-start.7 = (f32[26,10,1,128]{3,2,1,0:T(1,128)S(1)}, f32[26,10,1,128]{3,2,1,0:T(1,128)S(1)}, u32[]{:S(2)}, u32[]{:S(2)}) collective-permute-start(f32[26,10,1,128]{3,2,1,0:T(1,128)S(1)} %get-tuple-element.203), channel_id=1, source_target_pairs={{1,0},{0,1},{3,2},{2,3},{5,4},{4,5},{7,6},{6,7},{9,8},{8,9},{11,10... | collective-permute-start | bytes 399368 | tf_op jit(solution)/shard_map/ppermute | solution.py:47
  64.2 19.0 %collective-permute-start.8 = (f32[26,1,32,128]{3,2,1,0:T(8,128)S(1)}, f32[26,1,32,128]{3,2,1,0:T(8,128)S(1)}, u32[]{:S(2)}, u32[]{:S(2)}) collective-permute-start(f32[26,1,32,128]{3,2,1,0:T(8,128)S(1)} %get-tuple-element.220), channel_id=1, source_target_pairs={{0,2},{2,4},{4,6},{6,8},{8,10},{10,12},{12,14},{14,0},{1,3},{3,5},... | collective-permute-start | bytes 1277960 | tf_op jit(solution)/shard_map/ppermute | solution.py:46
  64.2 22.1 %collective-permute-start.9 = (f32[26,1,32,128]{3,2,1,0:T(8,128)S(1)}, f32[26,1,32,128]{3,2,1,0:T(8,128)S(1)}, u32[]{:S(2)}, u32[]{:S(2)}) collective-permute-start(f32[26,1,32,128]{3,2,1,0:T(8,128)S(1)} %get-tuple-element.219), channel_id=1, source_target_pairs={{2,0},{4,2},{6,4},{8,6},{10,8},{12,10},{14,12},{0,14},{3,1},{5,3},... | collective-permute-start | bytes 1277960 | tf_op jit(solution)/shard_map/ppermute | solution.py:47
  86.5 1.4 %collective-permute-start.10 = (f32[26,10,1,128]{3,2,1,0:T(1,128)S(1)}, f32[26,10,1,128]{3,2,1,0:T(1,128)S(1)}, u32[]{:S(2)}, u32[]{:S(2)}) collective-permute-start(f32[26,10,1,128]{3,2,1,0:T(1,128)S(1)} %get-tuple-element.200), channel_id=1, source_target_pairs={{0,1},{1,0},{2,3},{3,2},{4,5},{5,4},{6,7},{7,6},{8,9},{9,8},{10,11... | collective-permute-start | bytes 399368 | tf_op jit(solution)/shard_map/ppermute | solution.py:46
  86.6 1.5 %collective-permute-start.11 = (f32[26,10,1,128]{3,2,1,0:T(1,128)S(1)}, f32[26,10,1,128]{3,2,1,0:T(1,128)S(1)}, u32[]{:S(2)}, u32[]{:S(2)}) collective-permute-start(f32[26,10,1,128]{3,2,1,0:T(1,128)S(1)} %get-tuple-element.199), channel_id=1, source_target_pairs={{1,0},{0,1},{3,2},{2,3},{5,4},{4,5},{7,6},{6,7},{9,8},{8,9},{11,10... | collective-permute-start | bytes 399368 | tf_op jit(solution)/shard_map/ppermute | solution.py:47
  89.9 0.8 copy-start.2
where the time goes:
time: 91.7 us; the launch traced here: 91.5 us
  waiting for transfers between devices  51.7 us (56%)
  other arithmetic  18.4 us (20%)
  starting transfers between devices  17.3 us (19%)
  local copies, waits for them, and re-layouts  3.26 us (4%)
    ppermute x6, waiting for transfers between devices, extended_2(): before = lax.ppermute(last, axis, up)  43 us
    ppermute x6, starting transfers between devices, extended_2(): after = lax.ppermute(initial, axis, down)  13.7 us
    unnamed x79, other arithmetic  9.98 us
    ppermute x6, waiting for transfers between devices, extended_2(): after = lax.ppermute(initial, axis, down)  8.76 us
    mul x6, other arithmetic, finish(): loss = flow_loss * FLOW_WEIGHT[q] if q < 19 else salt_loss  4.3 us
    ppermute x6, starting transfers between devices, extended_2(): before = lax.ppermute(last, axis, up)  3.6 us
  transfers between devices with their start and end apart: 12, of which 12 were waited for; matrix products, arithmetic and copies ran while one was open for 3% of the time, Pallas kernels for 0%

commit v1 on v0

v1 whole, which is shorter than its diff:
```python
import functools

import jax
import jax.numpy as jnp
from jax import lax
from jax.experimental import pallas as pl
from jax.experimental.pallas import tpu as pltpu
from jax.sharding import PartitionSpec as P

MESH = pl.DeviceIdType.MESH
STEPS = 3

VELOCITY = [
    (0, 0, 0),
    (1, 0, 0),
    (-1, 0, 0),
    (0, 1, 0),
    (0, -1, 0),
    (0, 0, 1),
    (0, 0, -1),
    (1, 1, 0),
    (-1, -1, 0),
    (1, -1, 0),
    (-1, 1, 0),
    (1, 0, 1),
    (-1, 0, -1),
    (1, 0, -1),
    (-1, 0, 1),
    (0, 1, 1),
    (0, -1, -1),
    (0, 1, -1),
    (0, -1, 1),
]
VECTORS = VELOCITY + VELOCITY[:7]
FLOW_WEIGHT = [1.0 / 3.0] + [1.0 / 18.0] * 6 + [1.0 / 36.0] * 12
tau_plus = 0.65
tau_minus = 0.5 + 0.25 / (tau_plus - 0.5)
salt_minus = 0.7
salt_plus = 0.5 + 0.25 / (salt_minus - 0.5)
speed_scale = 0.1

ORDER = [9, 1, 11, 13, 20, 7, 3, 15, 17, 22, 10, 2, 12, 14, 21, 8, 4, 16, 18, 23]
ORDER += [0, 5, 6, 19, 24, 25]
SLOT = [ORDER.index(q) for q in range(26)]
SLANTED = [(11, 12), (14, 13), (15, 16), (18, 17)]
ROW = 8


def collide(f, flags):
    solid = (flags & 1) == 1
    open_wall = jnp.where(solid, 0.0, (flags >> 1).astype(jnp.float32))
    both = {q: f[q] + f[q + 1] for q in (*range(1, 19, 2), 20, 22, 24)}
    diff = {q: f[q] - f[q + 1] for q in (*range(1, 19, 2), 20, 22, 24)}
    density = f[0] + (
        ((both[1] + both[3]) + (both[5] + both[7]))
        + ((both[9] + both[11]) + (both[13] + both[15]))
        + both[17]
    )
    flux = [
        (diff[1] + diff[7]) + (diff[9] + diff[11]) + diff[13],
        (diff[3] + diff[7]) + (diff[15] + diff[17]) - diff[9],
        (diff[5] + diff[11]) + (diff[15] - diff[13]) - diff[17],
    ]
    inverse = 1.0 / density
    speed = [j * inverse for j in flux]
    rest = density - 1.5 * (flux[0] * speed[0] + flux[1] * speed[1] + flux[2] * speed[2])
    scaled = [4.5 * u for u in speed]

    def along(vec, values):
        total = None
        for sign, value in zip(vec, values):
            if sign == 0:
                continue
            if total is None:
                total = value
            else:
                total = total + value if sign > 0 else total - value
        return total

    post = [None] * 26
    post[0] = f[0] * (1.0 - 1.0 / tau_plus) + rest * (1.0 / (3.0 * tau_plus))
    for q in range(1, 19, 2):
        vec, weight = VELOCITY[q], FLOW_WEIGHT[q]
        j = along(vec, flux)
        even = j * along(vec, scaled) + rest
        dplus = both[q] * (0.5 / tau_plus) - even * (weight / tau_plus)
        dminus = diff[q] * (0.5 / tau_minus) - j * (3.0 * weight / tau_minus)
        post[q] = (f[q] - dplus) - dminus
        post[q + 1] = (f[q + 1] - dplus) + dminus
    conc = f[19] + ((both[20] + both[22]) + both[24])
    post[19] = f[19] * (1.0 - 1.0 / salt_plus) + conc * (0.25 / salt_plus)
    even = conc * (0.125 / salt_plus)
    for a in range(3):
        q = 20 + 2 * a
        dplus = both[q] * (0.5 / salt_plus) - even
        dminus = (diff[q] - conc * speed[a]) * (0.5 / salt_minus)
        post[q] = (f[q] - dplus) - dminus
        post[q + 1] = (f[q + 1] - dplus) + dminus
    for first in (*range(1, 19, 2), 20, 22, 24):
        post[first] = jnp.where(solid, f[first + 1], post[first])
        post[first + 1] = jnp.where(solid, f[first], post[first + 1])
    post[0] = jnp.where(solid, f[0], post[0])
    post[19] = jnp.where(solid, f[19], post[19])
    flow_loss = density * ((0.27 - 0.09 * conc) * open_wall)
    salt_loss = (0.02 * conc) * open_wall
    return post, flow_loss, salt_loss


def kernel(
    sizes, pops, flags, out, state, flag, fields, post, enter, load_sem, out_sem, send_sem, recv_sem
):
    nx, ny = sizes
    n_tiles = ny // 8
    nz = state.shape[-1]
    last = nx - 1
    inner_rows, below, above = pl.ds(ROW, ny), ROW - 1, ROW + ny

    size_x, size_y = lax.axis_size("gx"), lax.axis_size("gy")
    gx, gy = lax.axis_index("gx"), lax.axis_index("gy")
    right, left = lax.rem(gx + 1, size_x), lax.rem(gx + size_x - 1, size_x)
    other = lax.rem(gy + 1, size_y)

    def load(i, x, n):
        return pltpu.make_async_copy(
            pops.at[:, pl.ds(x, n)], state.at[:, pl.ds(x, n)], load_sem.at[i]
        )

    flag_load = pltpu.make_async_copy(flags, flag, load_sem.at[3])
    loads = [load(0, 0, 1), load(1, last, 1), load(2, 1, nx - 2)]
    flag_load.start()
    for item in loads:
        item.start()

    barrier = pltpu.get_barrier_semaphore()
    partners = [(left, gy), (right, gy), (gx, other), (left, other), (right, other)]
    for px, py in partners:
        pl.semaphore_signal(
            barrier, inc=1, device_id={"gx": px, "gy": py}, device_id_type=MESH
        )

    lane = lax.broadcasted_iota(jnp.int32, (8, nz), 1)
    floor, ceiling = lane == 0, lane == nz - 1

    def copies(s):
        buf = post.at[s]

        def copy(i, src, dst, px, py):
            return pltpu.make_async_remote_copy(
                src_ref=buf.at[src],
                dst_ref=buf.at[dst],
                send_sem=send_sem.at[s, i],
                recv_sem=recv_sem.at[s, i],
                device_id={"gx": px, "gy": py},
                device_id_type=MESH,
            )

        def at(q, n, x, nxs, row, rows=1):
            return (pl.ds(SLOT[q], n), pl.ds(x, nxs), pl.ds(row, rows))

        top = ROW + ny - 1
        to_left = [
            copy(0, at(10, 6, 1, 1, ROW, ny), at(10, 6, nx + 1, 1, ROW, ny), left, gy),
            copy(1, at(10, 1, 1, 1, top), at(10, 1, nx + 1, 1, below), left, other),
            copy(2, at(8, 1, 1, 1, ROW), at(8, 1, nx + 1, 1, above), left, other),
        ]
        to_right = [
            copy(3, at(9, 6, nx, 1, ROW, ny), at(9, 6, 0, 1, ROW, ny), right, gy),
            copy(4, at(7, 1, nx, 1, top), at(7, 1, 0, 1, below), right, other),
            copy(5, at(9, 1, nx, 1, ROW), at(9, 1, 0, 1, above), right, other),
        ]
        to_other = [
            copy(6, at(7, 6, 1, nx, top), at(7, 6, 1, nx, below), gx, other),
            copy(7, at(8, 5, 1, nx, ROW), at(8, 5, 1, nx, above), gx, other),
            copy(8, at(9, 1, 1, nx, ROW), at(9, 1, 1, nx, above), gx, other),
        ]
        return to_left, to_right, to_other

    exchange = [copies(s) for s in range(STEPS)]

    def pull(s, x, t):
        f = []
        for q in range(26):
            ex, ey, ez = VECTORS[q]
            f.append(post[s, SLOT[q], x + (1 - ex), pl.ds(ROW + 8 * t - ey, 8), :])
        for i, (rising, falling) in enumerate(SLANTED):
            wall = enter[s, i, x, pl.ds(8 * t, 8), :]
            f[rising] = jnp.where(floor, wall, f[rising])
            f[falling] = jnp.where(ceiling, wall, f[falling])
        return f

    def advance(s, x, t):
        rows = pl.ds(8 * t, 8)
        if s == 0:
            f = [state[q, x, rows, :] for q in range(26)]
        else:
            f = pull(s - 1, x, t)
        new, flow_loss, salt_loss = collide(f, flag[x, rows, :])

        def up(value):
            return pltpu.roll(value, 1, 1)

        def down(value):
            return pltpu.roll(value, nz - 1, 1)

        for i, (rising, falling) in enumerate(SLANTED):
            wall = jnp.where(floor, new[falling], new[rising])
            enter[s, i, x, rows, :] = wall - FLOW_WEIGHT[rising] * flow_loss
            new[rising], new[falling] = up(new[rising]), down(new[falling])
        for rising, falling, loss in ((5, 6, FLOW_WEIGHT[5] * flow_loss), (24, 25, salt_loss)):
            low, high = new[falling] - loss, new[rising] - loss
            new[rising] = jnp.where(floor, low, up(new[rising]))
            new[falling] = jnp.where(ceiling, high, down(new[falling]))
        for q in range(26):
            post[s, SLOT[q], x + 1, pl.ds(ROW + 8 * t, 8), :] = new[q]

    def measure(x, t):
        f = pull(STEPS - 1, x, t)
        rows = pl.ds(8 * t, 8)
        fields[0, x, rows, :] = sum(f[1:19], f[0])
        for a in range(3):
            total = None
            for q in range(1, 19, 2):
                sign = VELOCITY[q][a]
                if sign:
                    term = f[q] - f[q + 1]
                    if total is None:
                        total = term if sign > 0 else -term
                    else:
                        total = total + term if sign > 0 else total - term
            fields[1 + a, x, rows, :] = total * (1.0 / speed_scale)
        fields[4, x, rows, :] = sum(f[20:], f[19])

    def planes(work, lo, hi, tiles):
        def body(x, carry):
            for t in tiles:
                work(x, t)
            return carry

        lax.fori_loop(lo, hi, body, 0)

    every = range(n_tiles)
    middle = range(1, n_tiles - 1)
    edge = (0, n_tiles - 1)

    work = functools.partial(advance, 0)
    flag_load.wait()
    loads[0].wait()
    planes(work, 0, 1, every)
    pl.semaphore_wait(barrier, len(partners))
    for item in exchange[0][0]:
        item.start()
    loads[1].wait()
    planes(work, last, nx, every)
    for item in exchange[0][1]:
        item.start()
    loads[2].wait()
    planes(work, 1, last, every)
    for item in exchange[0][2]:
        item.start()

    for s in range(1, STEPS + 1):
        work = functools.partial(advance, s) if s < STEPS else measure
        to_left, to_right, to_other = exchange[s - 1]
        planes(work, 1, last, middle)
        for item in to_other:
            item.wait_recv()
        planes(work, 1, last, edge)
        if s == STEPS:
            part = pl.ds(1, nx - 2)
            stores = [pltpu.make_async_copy(fields.at[:, part], out.at[:, part], out_sem.at[0])]
            stores[0].start()
        for item in to_right:
            item.wait_recv()
        planes(work, 0, 1, every)
        if s < STEPS:
            for item in exchange[s][0]:
                item.start()
        else:
            part = pl.ds(0, 1)
            stores.append(
                pltpu.make_async_copy(fields.at[:, part], out.at[:, part], out_sem.at[1])
            )
            stores[1].start()
        for item in to_left:
            item.wait_recv()
        planes(work, last, nx, every)
        if s < STEPS:
            for item in exchange[s][1] + exchange[s][2]:
                item.start()
        else:
            part = pl.ds(last, 1)
            stores.append(
                pltpu.make_async_copy(fields.at[:, part], out.at[:, part], out_sem.at[2])
            )
            stores[2].start()

    for group in exchange:
        for side in group:
            for item in side:
                item.wait_send()
    for item in stores:
        item.wait()


def per_device(populations, cell_flags):
    _, nx, ny, nz = populations.shape
    return pl.pallas_call(
        functools.partial(kernel, (nx, ny)),
        out_shape=jax.ShapeDtypeStruct((5, nx, ny, nz), jnp.float32),
        in_specs=[pl.BlockSpec(memory_space=pl.ANY)] * 2,
        out_specs=pl.BlockSpec(memory_space=pl.ANY),
        scratch_shapes=[
            pltpu.VMEM((26, nx, ny, nz), jnp.float32),
            pltpu.VMEM((nx, ny, nz), jnp.int32),
            pltpu.VMEM((5, nx, ny, nz), jnp.float32),
            pltpu.VMEM((STEPS, 26, nx + 2, ny + 2 * ROW, nz), jnp.float32),
            pltpu.VMEM((STEPS, 4, nx, ny, nz), jnp.float32),
            pltpu.SemaphoreType.DMA((4,)),
            pltpu.SemaphoreType.DMA((3,)),
            pltpu.SemaphoreType.DMA((STEPS, 9)),
            pltpu.SemaphoreType.DMA((STEPS, 9)),
        ],
        compiler_params=pltpu.CompilerParams(
            collective_id=0, has_side_effects=True, vmem_limit_bytes=52 * 2**20
        ),
        cost_estimate=pl.CostEstimate(
            flops=900 * nx * ny * nz, bytes_accessed=128 * nx * ny * nz, transcendentals=0
        ),
    )(populations, cell_flags)


def solution(mesh):
    return jax.shard_map(
        per_device,
        mesh=mesh,
        in_specs=(P("seg", "gx", "gy", None), P("gx", "gy", "seg")),
        out_specs=P("seg", "gx", "gy", None),
        check_vma=False,
    )
```

time: 91.7 us -> 25.9 us (0.28)
  waiting for transfers between devices: 51.7 us -> 0 us
  Pallas kernels: 0 us -> 24 us
  other arithmetic: 18.4 us -> 0 us
  starting transfers between devices: 17.3 us -> 0 us
  local copies, waits for them, and re-layouts: 3.26 us -> 1.74 us
    ppermute x12 -> x0, waiting for transfers between devices: 51.7 us -> none  [the longest x6 43 us: extended_2(): before = lax.ppermute(last, axis, up)]
    pallas_call x0 -> x1, Pallas kernels: none -> 24 us  [per_device(): pl.pallas_call(functools.partial(kernel, (nx, ny)), out_shape=jax.ShapeDt...]
    ppermute x12 -> x0, starting transfers between devices: 17.3 us -> none  [the longest x6 13.7 us: extended_2(): after = lax.ppermute(initial, axis, down)]
    unnamed x79 -> x0, other arithmetic: 9.98 us -> none
    mul x8 -> x0, other arithmetic: 4.72 us -> none  [the longest x6 4.3 us: finish(): loss = flow_loss * FLOW_WEIGHT[q] if q < 19 else salt_loss]
    sub x9 -> x0, other arithmetic: 1.62 us -> none  [the longest x5 1.05 us: finish(): entering = inner[opposite_of(q)][:, :, :1] - loss[:, :, :1]]
    slice x16 -> x0, local copies, waits for them, and re-layouts: 1.38 us -> none  [the longest x13 1.2 us: finish(): parts.append(jnp.concatenate([source[:, :, 1:], entering], axis=2))]
    another operation x4 -> x0, other arithmetic: 1.2 us -> none  [the longest x1 0.82 us: moments(): return jnp.stack([density] + momenta + [conc])]
  transfers between devices with their start and end apart: 12 -> 0, of which waited for: 12 -> 0; matrix products, arithmetic and copies ran while one was open for 3% -> 0% of each run, Pallas kernels for 0% -> 0%
where the time goes in v1:
time: 25.9 us; the launch traced here: 25.7 us
  Pallas kernels  24 us (93%)
  local copies, waits for them, and re-layouts  1.74 us (7%)
    pallas_call x1, Pallas kernels, per_device(): pl.pallas_call(functools.partial(kernel, (nx, ny)), out_shape=jax.ShapeDt...  24 us
    unnamed x3, local copies, waits for them, and re-layouts  1.74 us

profile of v1, /device:TPU:0, one launch (start us, length us, event | category | flops | bytes accessed | tf_op | source)
XLA Modules:
  0.0 25.7 jit_solution(8106286217341754590)
XLA Ops:
  0.0 0.0 copy-start
  0.0 0.9 %copy-done = s32[8,32,128]{2,1,0:T(8,128)S(1)} copy-done((s32[8,32,128]{2,1,0:T(8,128)S(1)}, s32[8,32,128]{2,1,0:T(8,128)}, u32[]{:S(2)}) %copy-start) | copy-done | bytes 131096
  0.9 24.0 %shard_map.28 = f32[5,8,32,128]{3,2,1,0:T(8,128)S(1)} custom-call(f32[26,8,32,128]{3,2,1,0:T(8,128)} %pops.1, s32[8,32,128]{2,1,0:T(8,128)S(1)} %copy-done), custom_call_target="tpu_custom_call" | custom-call | flops 29491200 | bytes 4194304 | tf_op jit(solution)/shard_map/pallas_call | solution.py:307
  24.9 0.8 %copy.4 = f32[5,8,32,128]{3,2,1,0:T(8,128)} copy(f32[5,8,32,128]{3,2,1,0:T(8,128)S(1)} %shard_map.28) | data formatting | bytes 1310720
Async XLA Ops:
  0.0 0.9 %copy-start = (s32[8,32,128]{2,1,0:T(8,128)S(1)}, s32[8,32,128]{2,1,0:T(8,128)}, u32[]{:S(2)}) copy-start(s32[8,32,128]{2,1,0:T(8,128)} %flags.1) | copy-start | bytes 393220

commit v2 on v1

--- a/solution.py
+++ b/solution.py
@@ -113,12 +113,18 @@
     n_tiles = ny // 8
     nz = state.shape[-1]
     last = nx - 1
-    inner_rows, below, above = pl.ds(ROW, ny), ROW - 1, ROW + ny
+    below, above = ROW - 1, ROW + ny
 
     size_x, size_y = lax.axis_size("gx"), lax.axis_size("gy")
     gx, gy = lax.axis_index("gx"), lax.axis_index("gy")
-    right, left = lax.rem(gx + 1, size_x), lax.rem(gx + size_x - 1, size_x)
+    odd = lax.rem(gx, 2)
+    far = lax.rem(gx + size_x - 1 + 2 * odd, size_x)
+    near = lax.rem(gx + 1 + size_x - 2 * odd, size_x)
     other = lax.rem(gy + 1, size_y)
+    far_x, near_x = odd * last, (1 - odd) * last
+
+    def tile(k):
+        return k + gy * (n_tiles - 1 - 2 * k)
 
     def load(i, x, n):
         return pltpu.make_async_copy(
@@ -126,13 +132,13 @@
         )
 
     flag_load = pltpu.make_async_copy(flags, flag, load_sem.at[3])
-    loads = [load(0, 0, 1), load(1, last, 1), load(2, 1, nx - 2)]
+    loads = [load(0, far_x, 1), load(1, near_x, 1), load(2, 1, nx - 2)]
     flag_load.start()
     for item in loads:
         item.start()
 
     barrier = pltpu.get_barrier_semaphore()
-    partners = [(left, gy), (right, gy), (gx, other), (left, other), (right, other)]
+    partners = [(far, gy), (near, gy), (gx, other), (far, other), (near, other)]
     for px, py in partners:
         pl.semaphore_signal(
             barrier, inc=1, device_id={"gx": px, "gy": py}, device_id_type=MESH
@@ -154,42 +160,59 @@
                 device_id_type=MESH,
             )
 
-        def at(q, n, x, nxs, row, rows=1):
-            return (pl.ds(SLOT[q], n), pl.ds(x, nxs), pl.ds(row, rows))
+        def at(slot, n, x, nxs, row, rows=1):
+            return (pl.ds(slot, n), pl.ds(x, nxs), pl.ds(row, rows))
 
         top = ROW + ny - 1
-        to_left = [
-            copy(0, at(10, 6, 1, 1, ROW, ny), at(10, 6, nx + 1, 1, ROW, ny), left, gy),
-            copy(1, at(10, 1, 1, 1, top), at(10, 1, nx + 1, 1, below), left, other),
-            copy(2, at(8, 1, 1, 1, ROW), at(8, 1, nx + 1, 1, above), left, other),
+
+        def side(i, positive, x, there):
+            group, halo = 10 - 10 * positive, (1 - positive) * (nx + 1)
+            up, down = group + 5 * positive, group + 5 * (1 - positive)
+            first, final = gy * up + (1 - gy) * down, gy * down + (1 - gy) * up
+            begin, end = ROW + gy * (ny - 1), ROW + (1 - gy) * (ny - 1)
+            beyond, before = ROW + ny - gy * (ny + 1), ROW - 1 + gy * (ny + 1)
+            parts = []
+            for k in range(n_tiles):
+                row = pl.multiple_of(ROW + 8 * tile(k), 8)
+                parts.append(
+                    copy(i + k, at(group, 6, x + 1, 1, row, 8), at(group, 6, halo, 1, row, 8), there, gy)
+                )
+            i += n_tiles
+            corners = [
+                copy(i, at(first, 1, x + 1, 1, begin), at(first, 1, halo, 1, beyond), there, other),
+                copy(i + 1, at(final, 1, x + 1, 1, end), at(final, 1, halo, 1, before), there, other),
+            ]
+            return parts, corners
+
+        n_side = n_tiles + 2
+        to_far = side(0, odd, far_x, far)
+        to_near = side(n_side, 1 - odd, near_x, near)
+        i = 2 * n_side
+        to_other = [
+            copy(i, at(5, 6, 1, nx, top), at(5, 6, 1, nx, below), gx, other),
+            copy(i + 1, at(15, 5, 1, nx, ROW), at(15, 5, 1, nx, above), gx, other),
+            copy(i + 2, at(0, 1, 1, nx, ROW), at(0, 1, 1, nx, above), gx, other),
         ]
-        to_right = [
-            copy(3, at(9, 6, nx, 1, ROW, ny), at(9, 6, 0, 1, ROW, ny), right, gy),
-            copy(4, at(7, 1, nx, 1, top), at(7, 1, 0, 1, below), right, other),
-            copy(5, at(9, 1, nx, 1, ROW), at(9, 1, 0, 1, above), right, other),
-        ]
-        to_other = [
-            copy(6, at(7, 6, 1, nx, top), at(7, 6, 1, nx, below), gx, other),
-            copy(7, at(8, 5, 1, nx, ROW), at(8, 5, 1, nx, above), gx, other),
-            copy(8, at(9, 1, 1, nx, ROW), at(9, 1, 1, nx, above), gx, other),
-        ]
-        return to_left, to_right, to_other
+        return to_far, to_near, to_other
 
     exchange = [copies(s) for s in range(STEPS)]
+
+    def tile_rows(t):
+        return pl.ds(pl.multiple_of(8 * t, 8), 8)
 
     def pull(s, x, t):
         f = []
         for q in range(26):
             ex, ey, ez = VECTORS[q]
-            f.append(post[s, SLOT[q], x + (1 - ex), pl.ds(ROW + 8 * t - ey, 8), :])
+            f.append(post[s, SLOT[q], x + (1 - ex), pl.ds(8 * t + (ROW - ey), 8), :])
         for i, (rising, falling) in enumerate(SLANTED):
-            wall = enter[s, i, x, pl.ds(8 * t, 8), :]
+            wall = enter[s, i, x, tile_rows(t), :]
             f[rising] = jnp.where(floor, wall, f[rising])
             f[falling] = jnp.where(ceiling, wall, f[falling])
         return f
 
     def advance(s, x, t):
-        rows = pl.ds(8 * t, 8)
+        rows = tile_rows(t)
         if s == 0:
             f = [state[q, x, rows, :] for q in range(26)]
         else:
@@ -211,11 +234,11 @@
             new[rising] = jnp.where(floor, low, up(new[rising]))
             new[falling] = jnp.where(ceiling, high, down(new[falling]))
         for q in range(26):
-            post[s, SLOT[q], x + 1, pl.ds(ROW + 8 * t, 8), :] = new[q]
+            post[s, SLOT[q], x + 1, pl.ds(pl.multiple_of(ROW + 8 * t, 8), 8), :] = new[q]
 
     def measure(x, t):
         f = pull(STEPS - 1, x, t)
-        rows = pl.ds(8 * t, 8)
+        rows = tile_rows(t)
         fields[0, x, rows, :] = sum(f[1:19], f[0])
         for a in range(3):
             total = None
@@ -242,62 +265,86 @@
     middle = range(1, n_tiles - 1)
     edge = (0, n_tiles - 1)
 
+    def start(items):
+        for item in items:
+            item.start()
+
+    def arrive(items):
+        for item in items:
+            item.wait_recv()
+
+    def send(side, k):
+        parts, corners = side
+        if k == 0:
+            corners[0].start()
+        parts[k].start()
+        if k == n_tiles - 1:
+            corners[1].start()
+
+    def receive(side, k):
+        parts, corners = side
+        if k == 0:
+            arrive([corners[0], parts[0]])
+        if k + 1 < n_tiles:
+            arrive([parts[k + 1]])
+        else:
+            arrive([corners[1]])
+
+    def store(i, x, n):
+        item = pltpu.make_async_copy(
+            fields.at[:, pl.ds(x, n)], out.at[:, pl.ds(x, n)], out_sem.at[i]
+        )
+        item.start()
+        return item
+
     work = functools.partial(advance, 0)
     flag_load.wait()
     loads[0].wait()
-    planes(work, 0, 1, every)
-    pl.semaphore_wait(barrier, len(partners))
-    for item in exchange[0][0]:
-        item.start()
+    for k in every:
+        work(far_x, tile(k))
+        if k == 0:
+            pl.semaphore_wait(barrier, len(partners))
+        send(exchange[0][0], k)
     loads[1].wait()
-    planes(work, last, nx, every)
-    for item in exchange[0][1]:
-        item.start()
+    for k in every:
+        work(near_x, tile(k))
+        send(exchange[0][1], k)
     loads[2].wait()
     planes(work, 1, last, every)
-    for item in exchange[0][2]:
-        item.start()
-
-    for s in range(1, STEPS + 1):
-        work = functools.partial(advance, s) if s < STEPS else measure
-        to_left, to_right, to_other = exchange[s - 1]
+    start(exchange[0][2])
+
+    for s in range(1, STEPS):
+        work = functools.partial(advance, s)
+        to_far, to_near, to_other = exchange[s - 1]
         planes(work, 1, last, middle)
-        for item in to_other:
-            item.wait_recv()
+        arrive(to_other)
         planes(work, 1, last, edge)
-        if s == STEPS:
-            part = pl.ds(1, nx - 2)
-            stores = [pltpu.make_async_copy(fields.at[:, part], out.at[:, part], out_sem.at[0])]
-            stores[0].start()
-        for item in to_right:
-            item.wait_recv()
-        planes(work, 0, 1, every)
-        if s < STEPS:
-            for item in exchange[s][0]:
-                item.start()
-        else:
-            part = pl.ds(0, 1)
-            stores.append(
-                pltpu.make_async_copy(fields.at[:, part], out.at[:, part], out_sem.at[1])
-            )
-            stores[1].start()
-        for item in to_left:
-            item.wait_recv()
-        planes(work, last, nx, every)
-        if s < STEPS:
-            for item in exchange[s][1] + exchange[s][2]:
-                item.start()
-        else:
-            part = pl.ds(last, 1)
-            stores.append(
-                pltpu.make_async_copy(fields.at[:, part], out.at[:, part], out_sem.at[2])
-            )
-            stores[2].start()
-
-    for group in exchange:
-        for side in group:
-            for item in side:
-                item.wait_send()
+        for k in every:
+            receive(to_near, k)
+            work(near_x, tile(k))
+            send(exchange[s][1], k)
+            receive(to_far, k)
+            work(far_x, tile(k))
+            send(exchange[s][0], k)
+        start(exchange[s][2])
+
+    to_far, to_near, to_other = exchange[STEPS - 1]
+    planes(measure, 1, last, middle)
+    arrive(to_other)
+    planes(measure, 1, last, edge)
+    stores = [store(0, 1, nx - 2)]
+    for k in every:
+        receive(to_near, k)
+        measure(near_x, tile(k))
+    stores.append(store(1, near_x, 1))
+    for k in every:
+        receive(to_far, k)
+        measure(far_x, tile(k))
+    stores.append(store(2, far_x, 1))
+
+    for to_far, to_near, to_other in exchange:
+        for item in (*to_far[0], *to_far[1], *to_near[0], *to_near[1], *to_other):
+            item.wait_send()
     for item in stores:
         item.wait()
 
@@ -307,8 +354,8 @@
     return pl.pallas_call(
         functools.partial(kernel, (nx, ny)),
         out_shape=jax.ShapeDtypeStruct((5, nx, ny, nz), jnp.float32),
-        in_specs=[pl.BlockSpec(memory_space=pl.ANY)] * 2,
-        out_specs=pl.BlockSpec(memory_space=pl.ANY),
+        in_specs=[pl.BlockSpec(memory_space=pltpu.HBM)] * 2,
+        out_specs=pl.BlockSpec(memory_space=pltpu.HBM),
         scratch_shapes=[
             pltpu.VMEM((26, nx, ny, nz), jnp.float32),
             pltpu.VMEM((nx, ny, nz), jnp.int32),
@@ -317,8 +364,8 @@
             pltpu.VMEM((STEPS, 4, nx, ny, nz), jnp.float32),
             pltpu.SemaphoreType.DMA((4,)),
             pltpu.SemaphoreType.DMA((3,)),
-            pltpu.SemaphoreType.DMA((STEPS, 9)),
-            pltpu.SemaphoreType.DMA((STEPS, 9)),
+            pltpu.SemaphoreType.DMA((STEPS, 2 * (ny // 8 + 2) + 3)),
+            pltpu.SemaphoreType.DMA((STEPS, 2 * (ny // 8 + 2) + 3)),
         ],
         compiler_params=pltpu.CompilerParams(
             collective_id=0, has_side_effects=True, vmem_limit_bytes=52 * 2**20
@@ -326,7 +373,7 @@
         cost_estimate=pl.CostEstimate(
             flops=900 * nx * ny * nz, bytes_accessed=128 * nx * ny * nz, transcendentals=0
         ),
-    )(populations, cell_flags)
+    )(populations, pltpu.with_memory_space_constraint(cell_flags, pltpu.HBM))
 
 
 def solution(mesh):

time: 25.9 us -> 23.9 us (0.923)
  Pallas kernels: 24 us -> 22.9 us
  local copies, waits for them, and re-layouts: 1.74 us -> 0.84 us
    pallas_call x1, Pallas kernels: 24 us -> 22.9 us  [per_device(): pl.pallas_call(functools.partial(kernel, (nx, ny)), out_shape=jax.ShapeDt...]
    unnamed x3 -> x1, local copies, waits for them, and re-layouts: 1.74 us -> 0.84 us
where the time goes in v2:
time: 23.9 us; the launch traced here: 23.7 us
  Pallas kernels  22.9 us (96%)
  local copies, waits for them, and re-layouts  0.84 us (4%)
    pallas_call x1, Pallas kernels, per_device(): pl.pallas_call(functools.partial(kernel, (nx, ny)), out_shape=jax.ShapeDt...  22.9 us
    unnamed x1, local copies, waits for them, and re-layouts  0.84 us

profile of v2, /device:TPU:0, one launch (start us, length us, event | category | flops | bytes accessed | tf_op | source)
XLA Modules:
  0.0 23.7 jit_solution(7289339582217156800)
XLA Ops:
  0.0 22.9 %shard_map.28 = f32[5,8,32,128]{3,2,1,0:T(8,128)S(1)} custom-call(f32[26,8,32,128]{3,2,1,0:T(8,128)} %pops.1, s32[8,32,128]{2,1,0:T(8,128)} %flags.1), custom_call_target="tpu_custom_call" | custom-call | flops 29491200 | bytes 4194304 | tf_op jit(solution)/shard_map/pallas_call | solution.py:354
  22.9 0.8 %copy.4 = f32[5,8,32,128]{3,2,1,0:T(8,128)} copy(f32[5,8,32,128]{3,2,1,0:T(8,128)S(1)} %shard_map.28) | data formatting | bytes 1310720

commit v3 on v2

--- a/solution.py
+++ b/solution.py
@@ -121,6 +121,7 @@
     far = lax.rem(gx + size_x - 1 + 2 * odd, size_x)
     near = lax.rem(gx + 1 + size_x - 2 * odd, size_x)
     other = lax.rem(gy + 1, size_y)
+    ahead = gx < 2
     far_x, near_x = odd * last, (1 - odd) * last
 
     def tile(k):
@@ -303,14 +304,23 @@
     for k in every:
         work(far_x, tile(k))
         if k == 0:
+            @pl.when(ahead)
+            def _():
+                loads[2].wait()
+                planes(work, 1, last, every)
+
             pl.semaphore_wait(barrier, len(partners))
         send(exchange[0][0], k)
     loads[1].wait()
     for k in every:
         work(near_x, tile(k))
         send(exchange[0][1], k)
-    loads[2].wait()
-    planes(work, 1, last, every)
+
+    @pl.when(jnp.logical_not(ahead))
+    def _():
+        loads[2].wait()
+        planes(work, 1, last, every)
+
     start(exchange[0][2])
 
     for s in range(1, STEPS):
@@ -320,12 +330,12 @@
         arrive(to_other)
         planes(work, 1, last, edge)
         for k in every:
+            receive(to_far, k)
+            work(far_x, tile(k))
+            send(exchange[s][0], k)
             receive(to_near, k)
             work(near_x, tile(k))
             send(exchange[s][1], k)
-            receive(to_far, k)
-            work(far_x, tile(k))
-            send(exchange[s][0], k)
         start(exchange[s][2])
 
     to_far, to_near, to_other = exchange[STEPS - 1]

time: 23.9 us -> 23.1 us (0.967)
  Pallas kernels: 22.9 us -> 22.1 us
    pallas_call x1, Pallas kernels: 22.9 us -> 22.1 us  [per_device(): pl.pallas_call(functools.partial(kernel, (nx, ny)), out_shape=jax.ShapeDt...]
where the time goes in v3:
time: 23.1 us; the launch traced here: 23 us
  Pallas kernels  22.1 us (96%)
  local copies, waits for them, and re-layouts  0.84 us (4%)
    pallas_call x1, Pallas kernels, per_device(): pl.pallas_call(functools.partial(kernel, (nx, ny)), out_shape=jax.ShapeDt...  22.1 us
    unnamed x1, local copies, waits for them, and re-layouts  0.84 us

profile of v3, /device:TPU:0, one launch (start us, length us, event | category | flops | bytes accessed | tf_op | source)
XLA Modules:
  0.0 23.0 jit_solution(8478577692035944448)
XLA Ops:
  0.0 22.1 %shard_map.28 = f32[5,8,32,128]{3,2,1,0:T(8,128)S(1)} custom-call(f32[26,8,32,128]{3,2,1,0:T(8,128)} %pops.1, s32[8,32,128]{2,1,0:T(8,128)} %flags.1), custom_call_target="tpu_custom_call" | custom-call | flops 29491200 | bytes 4194304 | tf_op jit(solution)/shard_map/pallas_call | solution.py:364
  22.1 0.8 %copy.4 = f32[5,8,32,128]{3,2,1,0:T(8,128)} copy(f32[5,8,32,128]{3,2,1,0:T(8,128)S(1)} %shard_map.28) | data formatting | bytes 1310720
